TPU v7x, 512 devices: a whole 4x4x16 slice. The times are simulated.
512 devices in a mesh: res: 64 (over y, z_lo, core), ch: 8 (over z_hi, x).
Axes of the slice: x: 4, y: 4, z: 16 (z_hi: 2, z_lo: 8; z = z_hi * 8 + z_lo), core: 2. Of those that a mesh axis runs over, the one named last changes fastest.
Arguments:
- pair_rep: bfloat16 [512, 512, 128], P('res', 'ch'), may hold values from -6 to 6
- pair_mask: int32 [512, 512], P('res', 'ch'), may hold values from 0 to 1, as said below
- norm_gain: float32 [128], replicated, may hold values from 0.1 to 1.9
- norm_bias: float32 [128], replicated, may hold values from -2.5 to 2.5
- left_proj: bfloat16 [128, 128], replicated, may hold values from -0.5 to 0.5
- left_gate: bfloat16 [128, 128], replicated, may hold values from -0.5 to 0.5
- right_proj: bfloat16 [128, 128], replicated, may hold values from -0.5 to 0.5
- right_gate: bfloat16 [128, 128], replicated, may hold values from -0.5 to 0.5
- gate_proj: bfloat16 [128, 128], replicated, may hold values from -0.5 to 0.5
- out_gain: float32 [128], replicated, may hold values from 0.1 to 1.9
- out_bias: float32 [128], replicated, may hold values from -2.5 to 2.5
- out_proj: bfloat16 [128, 128], replicated, may hold values from -0.5 to 0.5
Outputs:
- update: bfloat16 [512, 512, 128], P('res', 'ch')
Inputs may be any that keep to these rules, and one draw needn't show every extreme that they name: pair_mask[i, j] = v[i] v[j] for a 0/1 vector v over the 512 tokens; v is 0 for trailing padding after a length L between 384 and 448, and also for scattered unresolved tokens before L.
All inputs are finite; a program needn't handle non-finite values.
Results may differ from a plain program's by a relative error of at most 0.017.
Values may be sent and summed in bfloat16 or wider, within the bound.
No kernel may reach another device: no remote copies, remote signals or barrier semaphores. Data moves between devices by JAX's collectives and lax.ppermute only.
A program may use at most 64 MiB of HBM per device.

v0:
```python
import jax
import jax.numpy as jnp
from jax import lax
from jax.sharding import PartitionSpec as P


def layer_norm(values, gain, bias):
    mean = jnp.mean(values, axis=-1, keepdims=True)
    centred = values - mean
    spread = jnp.mean(centred * centred, axis=-1, keepdims=True)
    return centred * lax.rsqrt(spread + 1e-05) * gain + bias


def channel_norm(values, gain, bias):
    mean = jnp.mean(values, axis=0, keepdims=True)
    centred = values - mean
    spread = jnp.mean(centred * centred, axis=0, keepdims=True)
    return centred * lax.rsqrt(spread + 1e-05) * gain[:, None, None] + bias[:, None, None]


def on_device(
    pair_rep,
    pair_mask,
    norm_gain,
    norm_bias,
    left_proj,
    left_gate,
    right_proj,
    right_gate,
    gate_proj,
    out_gain,
    out_bias,
    out_proj,
):
    normed = layer_norm(pair_rep.astype(jnp.float32), norm_gain, norm_bias).astype(jnp.bfloat16)
    maskf = pair_mask.astype(jnp.float32)[None]

    def project(weight):
        return jnp.einsum("ikd,dh->hik", normed, weight, preferred_element_type=jnp.float32)

    left = (maskf * jax.nn.sigmoid(project(left_gate)) * project(left_proj)).astype(jnp.bfloat16)
    right = (maskf * jax.nn.sigmoid(project(right_gate)) * project(right_proj)).astype(jnp.bfloat16)
    partial_sums = jnp.einsum(
        "cik,cjk->cij",
        left,
        lax.all_gather(right, "res", axis=1, tiled=True),
        preferred_element_type=jnp.float32,
    )
    mixed = lax.psum_scatter(
        partial_sums.astype(jnp.bfloat16), "ch", scatter_dimension=2, tiled=True
    ).astype(jnp.float32)
    mixed_norm = channel_norm(mixed, out_gain, out_bias).astype(jnp.bfloat16)
    projected = jnp.einsum("hij,hd->ijd", mixed_norm, out_proj, preferred_element_type=jnp.float32)
    gating = jax.nn.sigmoid(
        jnp.einsum("ijd,de->ije", normed, gate_proj, preferred_element_type=jnp.float32)
    )
    return (gating * projected).astype(jnp.bfloat16)


def solution(mesh):
    placed = (
        P("res", "ch", None),
        P("res", "ch"),
        P(),
        P(),
        P(),
        P(),
        P(),
        P(),
        P(),
        P(),
        P(),
        P(),
    )
    return jax.shard_map(
        on_device, mesh=mesh, in_specs=placed, out_specs=P("res", "ch", None), check_vma=False
    )
```

profile of v0, /device:TPU:1, one launch (start us, length us, event | category | flops | bytes accessed | tf_op | source)
XLA Modules:
  0.0 305.5 jit_solution(13222028918072801887)
XLA Ops:
  6.5 1.1 convert_reduce_fusion.1
  7.6 1.2 fusion.24
  8.8 0.7 convert_element_type.29
  9.5 1.3 fusion.3
  10.8 1.9 fusion.14
  12.7 0.0 all-gather.2.cloned.1.call-update
  12.7 0.0 reduce-scatter.2.cloned.1.call-start
  12.7 1.3 fusion.7
  14.0 1.2 fusion.15
  15.2 0.2 copy.28
  15.4 130.5 %all-gather.2.cloned.1.call-done = bf16[128,512,64]{0,2,1:T(8,128)(2,1)} async-done(((bf16[128,8,64]{0,2,1:T(8,128)(2,1)}), bf16[128,512,64]{0,2,1:T(8,128)(2,1)}) %all-gather.2.cloned.1.call-update) | async-done | bytes 8388624 | tf_op jit(solution)/shard_map/all_gather | solution.py:46
  145.9 23.7 %copy.29 = bf16[128,512,64]{2,1,0:T(8,128)(2,1)} copy(bf16[128,512,64]{0,2,1:T(8,128)(2,1)} %all-gather.2.cloned.1.call-done) | data formatting | bytes 16777216 | tf_op jit(solution)/shard_map/all_gather | solution.py:46
  169.7 10.3 %convolution_convert_fusion = bf16[128,8,512]{2,1,0:T(8,128)(2,1)S(1)} fusion(bf16[128,8,64]{2,1,0:T(8,128)(2,1)S(1)} %copy.28, bf16[128,512,64]{2,1,0:T(8,128)(2,1)} %copy.29), kind=kOutput, calls=%fused_computation | convolution fusion | flops 67633152 | bytes 9568256 | tf_op jit(solution)/shard_map/cik,cjk->cij/dot_general | solution.py:43
  180.0 2.0 copy.30
  182.1 0.3 fusion.10
  182.4 111.8 %reduce-scatter.2.cloned.1.call-done = bf16[128,8,64]{0,1,2:T(8,128)(2,1)} async-done(((bf16[128,8,512]{0,1,2:T(8,128)(2,1)}), bf16[128,8,64]{0,1,2:T(8,128)(2,1)}) %reduce-scatter.2.cloned.1.call-update) | async-done | bytes 131088 | tf_op jit(solution)/shard_map/reduce_scatter | solution.py:49
  294.2 1.0 convert_reduce_fusion
  295.3 0.1 copy.31
  295.3 0.1 copy.32
  295.4 1.1 fusion.20
  296.6 0.1 copy.33
  296.6 0.1 copy.34
  296.7 1.1 fusion.23
  297.9 0.8 fusion.13
  (22 shorter events, 0.1 us)
Async XLA Ops:
  6.5 3.0 copy-start
  6.5 139.4 %all-gather.2.cloned.1.call-start = ((), (), s32[]{:S(2)}) async-start(), calls=%async_computation.1 | async-start | bytes 8519680 | tf_op jit(solution)/shard_map/all_gather | solution.py:46
  12.7 281.5 %reduce-scatter.2.cloned.1.call-start = ((), (), s32[]{:S(2)}) async-start(), calls=%async_computation.2 | async-start | bytes 1179648 | tf_op jit(solution)/shard_map/reduce_scatter | solution.py:49
  169.7 12.4 %copy-start.1 = (bf16[8,64,128]{2,1,0:T(8,128)(2,1)S(1)}, bf16[8,64,128]{2,1,0:T(8,128)(2,1)}, u32[]{:S(2)}) copy-start(bf16[8,64,128]{2,1,0:T(8,128)(2,1)} %param.12) | copy-start | bytes 393220
  169.7 12.4 %copy-start.3 = (f32[128]{0:T(128)S(1)}, f32[128]{0:T(128)}, u32[]{:S(2)}) copy-start(f32[128]{0:T(128)} %param.15) | copy-start | bytes 1540
  169.7 12.4 %copy-start.4 = (f32[128]{0:T(128)S(1)}, f32[128]{0:T(128)}, u32[]{:S(2)}) copy-start(f32[128]{0:T(128)} %param.14) | copy-start | bytes 1540
  169.7 12.4 %copy-start.7 = (bf16[128,128]{1,0:T(8,128)(2,1)S(1)}, bf16[128,128]{1,0:T(8,128)(2,1)}, u32[]{:S(2)}) copy-start(bf16[128,128]{1,0:T(8,128)(2,1)} %param.20) | copy-start | bytes 98308
  169.7 127.1 %copy-start.5 = (f32[128]{0:T(128)S(1)}, f32[128]{0:T(128)}, u32[]{:S(2)}) copy-start(f32[128]{0:T(128)} %param.22) | copy-start | bytes 1540
  169.7 127.0 %copy-start.6 = (f32[128]{0:T(128)S(1)}, f32[128]{0:T(128)}, u32[]{:S(2)}) copy-start(f32[128]{0:T(128)} %param.21) | copy-start | bytes 1540
  169.7 128.2 %copy-start.2 = (bf16[128,128]{1,0:T(8,128)(2,1)S(1)}, bf16[128,128]{1,0:T(8,128)(2,1)}, u32[]{:S(2)}) copy-start(bf16[128,128]{1,0:T(8,128)(2,1)} %param.23) | copy-start | bytes 98308
Sparse Core Ops, SparseCore 0:
  12.8 133.0 all-gather.1
  182.2 111.9 reduce-scatter.1
where the time goes:
time: 307 us; the launch traced here: 306 us
  waiting for transfers between devices  242 us (79%)
  local copies, waits for them, and re-layouts  26.3 us (9%)
  matrix products  17.1 us (6%)
  between operations  13.6 us (4%)
  other arithmetic  6.22 us (2%)
    all_gather x1, waiting for transfers between devices, on_device(): lax.all_gather(right, 'res', axis=1, tiled=True)  130 us
    reduce_scatter x1, waiting for transfers between devices, on_device(): lax.psum_scatter(partial_sums.astype(jnp.bfloat16), 'ch', scatter_dimensi...  112 us
    all_gather x1, local copies, waits for them, and re-layouts, on_device(): lax.all_gather(right, 'res', axis=1, tiled=True)  23.7 us
    dot_general x1, matrix products, on_device(): jnp.einsum('cik,cjk->cij', left, lax.all_gather(right, 'res', axis=1, til...  10.3 us
  transfers between devices with their start and end apart: 2, of which 2 were waited for; matrix products, arithmetic and copies ran while one was open for 1% of the time, Pallas kernels for 0%

commit v1 on v0

v1 whole, which is shorter than its diff:
```python
import jax
import jax.numpy as jnp
from jax import lax
from jax.experimental import pallas as pl
from jax.experimental.pallas import tpu as pltpu
from jax.sharding import Mesh
from jax.sharding import PartitionSpec as P

EPS = 1e-05
F32, BF16 = jnp.float32, jnp.bfloat16
VMEM_LIMIT = 32 * 1024 * 1024


def dot_last(a, b):
    return lax.dot_general(a, b, (((1,), (1,)), ((), ())), preferred_element_type=F32)


def call(kernel, outs, scratch, *args, flops=1 << 24):
    return pl.pallas_call(
        kernel,
        out_shape=outs,
        scratch_shapes=scratch,
        compiler_params=pltpu.CompilerParams(vmem_limit_bytes=VMEM_LIMIT),
    )(*args)


def prepare(x_ref, mask_ref, gain_ref, bias_ref, lp_ref, lg_ref, rp_ref, rg_ref, gate_ref, send_ref, gating_ref, rows):
    x = x_ref[...].astype(F32)
    mean = jnp.mean(x, axis=-1, keepdims=True)
    centred = x - mean
    spread = jnp.mean(centred * centred, axis=-1, keepdims=True)
    normed = (centred * lax.rsqrt(spread + EPS) * gain_ref[...] + bias_ref[...]).astype(BF16)

    def edge(proj_ref, gate_ref):
        value = dot_last(proj_ref[...].T, normed)
        gate = dot_last(gate_ref[...].T, normed)
        return jax.nn.sigmoid(gate) * value

    left = edge(lp_ref, lg_ref)
    right = edge(rp_ref, rg_ref)
    mask = mask_ref[...].astype(F32)
    mask = jnp.concatenate([mask, mask], axis=1)
    for i in range(8):
        at = slice(i * 64, (i + 1) * 64)
        both = jnp.concatenate([left[:, at], right[:, at]], axis=1)
        rows[:, i, :] = both * mask[i : i + 1, :]
    send_ref[...] = rows[...].reshape(1024, 128).astype(BF16)
    gating_ref[...] = jax.nn.sigmoid(jnp.dot(normed, gate_ref[...], preferred_element_type=F32))


def contract(own_ref, both_ref, send_ref, lhs, out):
    own = own_ref[...].astype(F32).reshape(32, 4, 8, 128)
    both = both_ref[...].astype(F32).reshape(2, 32, 4, 8, 128)
    for x in range(2):
        lhs[x] = jnp.concatenate([own[:, 2 * x, :, :64], own[:, 2 * x + 1, :, :64]], axis=-1).reshape(256, 128)
    parts = []
    for x in range(4):
        part = jnp.stack([both[0, :, x], both[1, :, x]], axis=1).reshape(512, 128)
        parts.append(part[:, 64:])
    rhs = jnp.concatenate(parts, axis=1).astype(BF16)
    mixed = []
    for e in range(2):
        halves = [lhs[x, pl.ds(e, 128, stride=2), :] for x in range(2)]
        mixed.append(dot_last(jnp.concatenate(halves, axis=1).astype(BF16), rhs))
    for h in range(8):
        at = slice(h * 64, (h + 1) * 64)
        tile = jnp.concatenate([mixed[0][:, at], mixed[1][:, at]], axis=1).reshape(16, 8, 128)
        out[:, 0, h * 4 : (h + 1) * 4, :] = tile[:, 0:4, :]
        out[:, 1, h * 4 : (h + 1) * 4, :] = tile[:, 4:8, :]
    send_ref[...] = out[...].reshape(1024, 128).astype(BF16)


def finish(got_ref, gating_ref, gain_ref, bias_ref, proj_ref, out_ref, rows):
    got = got_ref[...].astype(F32).reshape(32, 2, 16, 128)
    rows[...] = (got[:, 0] + got[:, 1]).reshape(512, 128)
    gain = jnp.broadcast_to(gain_ref[...], (128, 128)).T
    bias = jnp.broadcast_to(bias_ref[...], (128, 128)).T
    for a in range(4):
        mixed = rows[pl.ds(a, 128, stride=4), :]
        mean = jnp.mean(mixed, axis=0, keepdims=True)
        centred = mixed - mean
        spread = jnp.mean(centred * centred, axis=0, keepdims=True)
        normed = (centred * lax.rsqrt(spread + EPS) * gain + bias).astype(BF16)
        projected = lax.dot_general(normed, proj_ref[...], (((0,), (0,)), ((), ())), preferred_element_type=F32)
        at = slice(a * 128, (a + 1) * 128)
        out_ref[at, :] = (gating_ref[at, :] * projected).astype(BF16)


def on_device(
    pair_rep,
    pair_mask,
    norm_gain,
    norm_bias,
    left_proj,
    left_gate,
    right_proj,
    right_gate,
    gate_proj,
    out_gain,
    out_bias,
    out_proj,
):
    send, gating = call(
        prepare,
        (jax.ShapeDtypeStruct((1024, 128), BF16), jax.ShapeDtypeStruct((512, 128), F32)),
        [pltpu.VMEM((128, 8, 128), F32)],
        pair_rep.reshape(512, 128),
        pair_mask,
        norm_gain.reshape(1, 128),
        norm_bias.reshape(1, 128),
        left_proj,
        left_gate,
        right_proj,
        right_gate,
        gate_proj,
    )
    got = lax.all_to_all(send.reshape(128, 8, 128), ("y", "z_lo", "x"), 0, 0, tiled=True).reshape(1024, 128)
    both = lax.all_gather(got, "core", axis=0, tiled=True)
    send = call(
        contract,
        jax.ShapeDtypeStruct((1024, 128), BF16),
        [pltpu.VMEM((2, 256, 128), F32), pltpu.VMEM((16, 2, 32, 128), F32)],
        got,
        both,
    )
    got = lax.all_to_all(send.reshape(256, 4, 128), ("y", "z_lo", "z_hi", "x"), 0, 0, tiled=True).reshape(1024, 128)
    out = call(
        finish,
        jax.ShapeDtypeStruct((512, 128), BF16),
        [pltpu.VMEM((512, 128), F32)],
        got,
        gating,
        out_gain.reshape(1, 128),
        out_bias.reshape(1, 128),
        out_proj,
    )
    return out.reshape(8, 64, 128)


def solution(mesh):
    fine = Mesh(mesh.devices.reshape(4, 8, 2, 2, 4), ("y", "z_lo", "core", "z_hi", "x"))
    res, ch = ("y", "z_lo", "core"), ("z_hi", "x")
    placed = (P(res, ch, None), P(res, ch)) + (P(),) * 10
    return jax.shard_map(on_device, mesh=fine, in_specs=placed, out_specs=P(res, ch, None), check_vma=False)
```

time: 307 us -> 88.1 us (0.29)
  the two profiles are of different devices: /device:TPU:1 before, /device:TPU:32 now
where the time goes in v1:
time: 88.1 us; the launch traced here: 87.4 us
  blocking collectives  79 us (90%)
  local copies, waits for them, and re-layouts  6.05 us (7%)
  Pallas kernels  2.4 us (3%)
    all_to_all x1, blocking collectives, on_device(): lax.all_to_all(send.reshape(128, 8, 128), ('y', 'z_lo', 'x'), 0, 0, tiled...  39.1 us
    all_to_all x1, blocking collectives, on_device(): lax.all_to_all(send.reshape(256, 4, 128), ('y', 'z_lo', 'z_hi', 'x'), 0,...  37.7 us
    unnamed x24, local copies, waits for them, and re-layouts  6.05 us
    pallas_call x3, Pallas kernels, call(): pl.pallas_call(kernel, out_shape=outs, scratch_shapes=scratch, compiler_p...  2.4 us
    all_gather x1, blocking collectives, on_device(): both = lax.all_gather(got, 'core', axis=0, tiled=True)  2.17 us

profile of v1, /device:TPU:32, one launch (start us, length us, event | category | flops | bytes accessed | tf_op | source)
XLA Modules:
  0.0 87.4 jit_solution(16073219900178534018)
XLA Ops:
  0.0 0.0 copy-start.8
  0.0 0.0 copy-start.9
  0.0 0.7 copy-done.7
  0.7 0.0 copy-done.8
  0.7 0.0 copy-done.9
  0.7 0.0 copy-start
  0.7 0.9 %copy-done = bf16[8,64,128]{2,1,0:T(8,128)(2,1)S(1)} copy-done((bf16[8,64,128]{2,1,0:T(8,128)(2,1)S(1)}, bf16[8,64,128]{2,1,0:T(8,128)(2,1)}, u32[]{:S(2)}) %copy-start) | copy-done | bytes 131096
  1.6 0.0 copy-start.1
  1.6 0.8 copy-done.1
  2.4 0.0 copy-start.2
  2.4 0.8 copy-done.2
  3.1 0.8 copy-done.3
  3.9 0.8 copy-done.4
  4.6 0.8 copy-done.5
  5.4 0.9 %shard_map.118 = (bf16[1024,128]{1,0:T(8,128)(2,1)S(1)}, f32[512,128]{1,0:T(8,128)S(1)}) custom-call(bf16[512,128]{1,0:T(8,128)(2,1)S(1)} %bitcast.15, s32[8,64]{1,0:T(8,128)S(1)} %copy-done.7, f32[1,128]{1,0:T(1,128)S(1)} %bitcast.16, f32[1,128]{1,0:T(1,128)S(1)} %bitcast.17, bf16[128,128]{1,0:T(8,128)(2,1)S(1)} %copy-done.1, ...), custom_call_target="tpu_custom_call" | custom-call | tf_op jit(solution)/shard_map/pallas_call | solution.py:19
  6.3 39.1 %all_to_all.10 = bf16[128,8,128]{2,1,0:T(8,128)(2,1)S(1)} all-to-all(bf16[128,8,128]{2,1,0:T(8,128)(2,1)S(1)} %bitcast.14), channel_id=1, replica_groups=mesh['y'=4,'z_lo'=8,'core'=2,'z_hi'=2,'x'=4] {'y','z_lo','x'}, dimensions={0} | all-to-all | bytes 524288 | tf_op jit(solution)/shard_map/all_to_all | solution.py:117
  45.4 2.2 %all_gather.3.both_ref = bf16[2048,128]{1,0:T(8,128)(2,1)S(1)} all-gather(bf16[1024,128]{1,0:T(8,128)(2,1)S(1)} %bitcast.10), channel_id=1, replica_groups=mesh['y'=4,'z_lo'=8,'core'=2,'z_hi'=2,'x'=4] {'core'}, dimensions={0}, use_global_device_ids=true | all-gather | bytes 786432 | tf_op jit(solution)/shard_map/all_gather | solution.py:118
  47.5 0.5 shard_map.119
  48.1 0.0 copy-start.6
  48.1 37.7 %all_to_all.11 = bf16[256,4,128]{2,1,0:T(4,128)(2,1)S(1)} all-to-all(bf16[256,4,128]{2,1,0:T(4,128)(2,1)S(1)} %bitcast.13), channel_id=1, replica_groups=mesh['y'=4,'z_lo'=8,'core'=2,'z_hi'=2,'x'=4] {'y','z_lo','z_hi','x'}, dimensions={0} | all-to-all | bytes 524288 | tf_op jit(solution)/shard_map/all_to_all | solution.py:126
  85.8 0.0 copy-done.6
  85.8 0.6 copy-done.10
  86.4 0.0 copy-done.11
  86.5 1.0 %shard_map.120 = bf16[512,128]{1,0:T(8,128)(2,1)} custom-call(bf16[1024,128]{1,0:T(8,128)(2,1)S(1)} %bitcast.12, f32[512,128]{1,0:T(8,128)S(1)} %get-tuple-element.8.gating_ref, f32[1,128]{1,0:T(1,128)S(1)} %bitcast.18, f32[1,128]{1,0:T(1,128)S(1)} %bitcast.19, bf16[128,128]{1,0:T(8,128)(2,1)S(1)} %copy-done.6), custom_call_target="tpu_custom_call" | custom-call | tf_op jit(solution)/shard_map/pallas_call | solution.py:19
  (6 shorter events, 0.0 us)
Async XLA Ops:
  0.0 0.7 copy-start.7
  0.0 0.7 copy-start.8
  0.0 0.7 copy-start.9
  0.7 0.9 %copy-start = (bf16[8,64,128]{2,1,0:T(8,128)(2,1)S(1)}, bf16[8,64,128]{2,1,0:T(8,128)(2,1)}, u32[]{:S(2)}) copy-start(bf16[8,64,128]{2,1,0:T(8,128)(2,1)} %param.12) | copy-start | bytes 393220
  1.6 0.8 copy-start.1
  2.4 0.8 copy-start.2
  3.1 0.8 copy-start.3
  3.9 0.8 copy-start.4
  4.6 0.8 copy-start.5
  48.1 37.7 %copy-start.6 = (bf16[128,128]{1,0:T(8,128)(2,1)S(1)}, bf16[128,128]{1,0:T(8,128)(2,1)}, u32[]{:S(2)}) copy-start(bf16[128,128]{1,0:T(8,128)(2,1)} %proj_ref.1) | copy-start | bytes 98308
  85.8 0.7 copy-start.10
  85.8 0.7 copy-start.11

commit v2 on v1

--- a/solution.py
+++ b/solution.py
@@ -15,21 +15,31 @@
     return lax.dot_general(a, b, (((1,), (1,)), ((), ())), preferred_element_type=F32)
 
 
-def call(kernel, outs, scratch, *args, flops=1 << 24):
+def call(kernel, outs, scratch, *args, space=pltpu.VMEM, limit=VMEM_LIMIT):
     return pl.pallas_call(
         kernel,
         out_shape=outs,
+        in_specs=[pl.BlockSpec(memory_space=space)] * len(args),
         scratch_shapes=scratch,
-        compiler_params=pltpu.CompilerParams(vmem_limit_bytes=VMEM_LIMIT),
+        compiler_params=pltpu.CompilerParams(vmem_limit_bytes=limit),
     )(*args)
 
 
-def prepare(x_ref, mask_ref, gain_ref, bias_ref, lp_ref, lg_ref, rp_ref, rg_ref, gate_ref, send_ref, gating_ref, rows):
+def prepare(*refs):
+    sources, (send_ref, gating_ref, affine_ref, last_ref, rows), held, sems = refs[:12], refs[12:17], refs[17:29], refs[29]
+    copies = [pltpu.make_async_copy(s, h, sems.at[n]) for n, (s, h) in enumerate(zip(sources, held))]
+    for copy in copies:
+        copy.start()
+    x_ref, mask_ref, gain_ref, bias_ref, lp_ref, lg_ref, rp_ref, rg_ref, gate_ref, og_ref, ob_ref, op_ref = held
+    copies[0].wait()
     x = x_ref[...].astype(F32)
     mean = jnp.mean(x, axis=-1, keepdims=True)
     centred = x - mean
     spread = jnp.mean(centred * centred, axis=-1, keepdims=True)
-    normed = (centred * lax.rsqrt(spread + EPS) * gain_ref[...] + bias_ref[...]).astype(BF16)
+    scaled = centred * lax.rsqrt(spread + EPS)
+    for copy in copies[1:]:
+        copy.wait()
+    normed = (scaled * gain_ref[...] + bias_ref[...]).astype(BF16)
 
     def edge(proj_ref, gate_ref):
         value = dot_last(proj_ref[...].T, normed)
@@ -46,6 +56,9 @@
         rows[:, i, :] = both * mask[i : i + 1, :]
     send_ref[...] = rows[...].reshape(1024, 128).astype(BF16)
     gating_ref[...] = jax.nn.sigmoid(jnp.dot(normed, gate_ref[...], preferred_element_type=F32))
+    affine_ref[0] = jnp.broadcast_to(og_ref[...], (128, 128)).T
+    affine_ref[1] = jnp.broadcast_to(ob_ref[...], (128, 128)).T
+    last_ref[...] = op_ref[...]
 
 
 def contract(own_ref, both_ref, send_ref, lhs, out):
@@ -70,17 +83,15 @@
     send_ref[...] = out[...].reshape(1024, 128).astype(BF16)
 
 
-def finish(got_ref, gating_ref, gain_ref, bias_ref, proj_ref, out_ref, rows):
+def finish(got_ref, gating_ref, affine_ref, proj_ref, out_ref, rows):
     got = got_ref[...].astype(F32).reshape(32, 2, 16, 128)
     rows[...] = (got[:, 0] + got[:, 1]).reshape(512, 128)
-    gain = jnp.broadcast_to(gain_ref[...], (128, 128)).T
-    bias = jnp.broadcast_to(bias_ref[...], (128, 128)).T
     for a in range(4):
         mixed = rows[pl.ds(a, 128, stride=4), :]
         mean = jnp.mean(mixed, axis=0, keepdims=True)
         centred = mixed - mean
         spread = jnp.mean(centred * centred, axis=0, keepdims=True)
-        normed = (centred * lax.rsqrt(spread + EPS) * gain + bias).astype(BF16)
+        normed = (centred * lax.rsqrt(spread + EPS) * affine_ref[0] + affine_ref[1]).astype(BF16)
         projected = lax.dot_general(normed, proj_ref[...], (((0,), (0,)), ((), ())), preferred_element_type=F32)
         at = slice(a * 128, (a + 1) * 128)
         out_ref[at, :] = (gating_ref[at, :] * projected).astype(BF16)
@@ -100,10 +111,7 @@
     out_bias,
     out_proj,
 ):
-    send, gating = call(
-        prepare,
-        (jax.ShapeDtypeStruct((1024, 128), BF16), jax.ShapeDtypeStruct((512, 128), F32)),
-        [pltpu.VMEM((128, 8, 128), F32)],
+    operands = (
         pair_rep.reshape(512, 128),
         pair_mask,
         norm_gain.reshape(1, 128),
@@ -113,6 +121,24 @@
         right_proj,
         right_gate,
         gate_proj,
+        out_gain.reshape(1, 128),
+        out_bias.reshape(1, 128),
+        out_proj,
+    )
+    send, gating, affine, last = call(
+        prepare,
+        (
+            jax.ShapeDtypeStruct((1024, 128), BF16),
+            jax.ShapeDtypeStruct((512, 128), F32),
+            jax.ShapeDtypeStruct((2, 128, 128), F32),
+            jax.ShapeDtypeStruct((128, 128), BF16),
+        ),
+        [pltpu.VMEM((128, 8, 128), F32)]
+        + [pltpu.VMEM(o.shape, o.dtype) for o in operands]
+        + [pltpu.SemaphoreType.DMA((len(operands),))],
+        *operands,
+        space=pltpu.HBM,
+        limit=64 * 1024 * 1024 - 512 * 1024,
     )
     got = lax.all_to_all(send.reshape(128, 8, 128), ("y", "z_lo", "x"), 0, 0, tiled=True).reshape(1024, 128)
     both = lax.all_gather(got, "core", axis=0, tiled=True)
@@ -130,9 +156,8 @@
         [pltpu.VMEM((512, 128), F32)],
         got,
         gating,
-        out_gain.reshape(1, 128),
-        out_bias.reshape(1, 128),
-        out_proj,
+        affine,
+        last,
     )
     return out.reshape(8, 64, 128)
 

time: 88.1 us -> 83.9 us (0.952)
  the two profiles are of different devices: /device:TPU:32 before, /device:TPU:1 now
where the time goes in v2:
time: 83.9 us; the launch traced here: 82.3 us
  blocking collectives  77.9 us (93%)
  Pallas kernels  4.29 us (5%)
    all_to_all x1, blocking collectives, on_device(): lax.all_to_all(send.reshape(128, 8, 128), ('y', 'z_lo', 'x'), 0, 0, tiled...  40.8 us
    all_to_all x1, blocking collectives, on_device(): lax.all_to_all(send.reshape(256, 4, 128), ('y', 'z_lo', 'z_hi', 'x'), 0,...  33.5 us
    pallas_call x3, Pallas kernels, call(): pl.pallas_call(kernel, out_shape=outs, in_specs=[pl.BlockSpec(memory_spac...  4.29 us
    all_gather x1, blocking collectives, on_device(): both = lax.all_gather(got, 'core', axis=0, tiled=True)  3.59 us

profile of v2, /device:TPU:1, one launch (start us, length us, event | category | flops | bytes accessed | tf_op | source)
XLA Modules:
  0.0 82.3 jit_solution(572443084301421878)
XLA Ops:
  0.0 2.8 %shard_map.118 = (bf16[1024,128]{1,0:T(8,128)(2,1)}, f32[512,128]{1,0:T(8,128)}, f32[2,128,128]{2,1,0:T(8,128)}, bf16[128,128]{1,0:T(8,128)(2,1)}) custom-call(bf16[512,128]{1,0:T(8,128)(2,1)} %bitcast.15, s32[8,64]{1,0:T(8,128)} %refs_1_.1, f32[1,128]{1,0:T(1,128)} %bitcast.16, f32[1,128]{1,0:T(1,128)} %bitcast.17, bf16[128,128]{1,0:T(8,128)(2,1)} %refs_4_.1, ...), custom_call_target="tpu_custom_call" | custom-call | tf_op jit(solution)/shard_map/pallas_call | solution.py:19
  2.8 40.8 %all_to_all.10 = bf16[128,8,128]{2,1,0:T(8,128)(2,1)S(1)} all-to-all(bf16[128,8,128]{2,1,0:T(8,128)(2,1)} %bitcast.14), channel_id=1, replica_groups=mesh['y'=4,'z_lo'=8,'core'=2,'z_hi'=2,'x'=4] {'y','z_lo','x'}, dimensions={0} | all-to-all | bytes 524288 | tf_op jit(solution)/shard_map/all_to_all | solution.py:143
  43.5 3.6 %all_gather.3.both_ref = bf16[2048,128]{1,0:T(8,128)(2,1)S(1)} all-gather(bf16[1024,128]{1,0:T(8,128)(2,1)S(1)} %bitcast.10), channel_id=1, replica_groups=mesh['y'=4,'z_lo'=8,'core'=2,'z_hi'=2,'x'=4] {'core'}, dimensions={0}, use_global_device_ids=true | all-gather | bytes 786432 | tf_op jit(solution)/shard_map/all_gather | solution.py:144
  47.1 0.5 shard_map.119
  47.7 0.0 copy-start
  47.7 0.0 copy-start.1
  47.7 0.0 copy-start.2
  47.7 33.5 %all_to_all.11 = bf16[256,4,128]{2,1,0:T(4,128)(2,1)S(1)} all-to-all(bf16[256,4,128]{2,1,0:T(4,128)(2,1)S(1)} %bitcast.13), channel_id=1, replica_groups=mesh['y'=4,'z_lo'=8,'core'=2,'z_hi'=2,'x'=4] {'y','z_lo','z_hi','x'}, dimensions={0} | all-to-all | bytes 524288 | tf_op jit(solution)/shard_map/all_to_all | solution.py:152
  81.3 0.0 copy-done
  81.3 0.0 copy-done.1
  81.3 0.0 copy-done.2
  81.3 1.0 %shard_map.120 = bf16[512,128]{1,0:T(8,128)(2,1)} custom-call(bf16[1024,128]{1,0:T(8,128)(2,1)S(1)} %bitcast.12, f32[512,128]{1,0:T(8,128)S(1)} %copy-done, f32[2,128,128]{2,1,0:T(8,128)S(1)} %copy-done.1, bf16[128,128]{1,0:T(8,128)(2,1)S(1)} %copy-done.2), custom_call_target="tpu_custom_call" | custom-call | tf_op jit(solution)/shard_map/pallas_call | solution.py:19
Async XLA Ops:
  47.7 33.6 %copy-start = (f32[512,128]{1,0:T(8,128)S(1)}, f32[512,128]{1,0:T(8,128)}, u32[]{:S(2)}) copy-start(f32[512,128]{1,0:T(8,128)} %get-tuple-element.10.gating_ref) | copy-start | bytes 786436
  47.7 33.6 %copy-start.1 = (f32[2,128,128]{2,1,0:T(8,128)S(1)}, f32[2,128,128]{2,1,0:T(8,128)}, u32[]{:S(2)}) copy-start(f32[2,128,128]{2,1,0:T(8,128)} %get-tuple-element.11.affine_ref) | copy-start | bytes 393220
  47.7 33.6 %copy-start.2 = (bf16[128,128]{1,0:T(8,128)(2,1)S(1)}, bf16[128,128]{1,0:T(8,128)(2,1)}, u32[]{:S(2)}) copy-start(bf16[128,128]{1,0:T(8,128)(2,1)} %get-tuple-element.12.proj_ref) | copy-start | bytes 98308

commit v3 on v2

--- a/solution.py
+++ b/solution.py
@@ -62,13 +62,13 @@
 
 
 def contract(own_ref, both_ref, send_ref, lhs, out):
-    own = own_ref[...].astype(F32).reshape(32, 4, 8, 128)
-    both = both_ref[...].astype(F32).reshape(2, 32, 4, 8, 128)
+    own = own_ref[...].astype(F32).reshape(4, 4, 64, 128)
+    both = both_ref[...].astype(F32).reshape(2, 4, 4, 8, 8, 128)
     for x in range(2):
         lhs[x] = jnp.concatenate([own[:, 2 * x, :, :64], own[:, 2 * x + 1, :, :64]], axis=-1).reshape(256, 128)
     parts = []
     for x in range(4):
-        part = jnp.stack([both[0, :, x], both[1, :, x]], axis=1).reshape(512, 128)
+        part = jnp.stack([both[0, :, x], both[1, :, x]], axis=2).reshape(512, 128)
         parts.append(part[:, 64:])
     rhs = jnp.concatenate(parts, axis=1).astype(BF16)
     mixed = []
@@ -77,15 +77,25 @@
         mixed.append(dot_last(jnp.concatenate(halves, axis=1).astype(BF16), rhs))
     for h in range(8):
         at = slice(h * 64, (h + 1) * 64)
-        tile = jnp.concatenate([mixed[0][:, at], mixed[1][:, at]], axis=1).reshape(16, 8, 128)
-        out[:, 0, h * 4 : (h + 1) * 4, :] = tile[:, 0:4, :]
-        out[:, 1, h * 4 : (h + 1) * 4, :] = tile[:, 4:8, :]
+        tile = jnp.concatenate([mixed[0][:, at], mixed[1][:, at]], axis=1).reshape(4, 4, 8, 128)
+        to = slice(h % 4 * 4, h % 4 * 4 + 4)
+        for y in range(4):
+            for s in range(2):
+                out[:, s, h // 4, y, to, :] = tile[y, :, 4 * s : 4 * s + 4, :]
     send_ref[...] = out[...].reshape(1024, 128).astype(BF16)
 
 
+def add_halves(got_ref, send_ref, out):
+    got = got_ref[...].astype(F32).reshape(8, 2, 64, 128)
+    for z in range(8):
+        total = (got[z, 0] + got[z, 1]).reshape(8, 8, 128)
+        for s in range(2):
+            out[:, s, z * 4 : z * 4 + 4, :] = total[:, 4 * s : 4 * s + 4, :]
+    send_ref[...] = out[...].reshape(512, 128).astype(BF16)
+
+
 def finish(got_ref, gating_ref, affine_ref, proj_ref, out_ref, rows):
-    got = got_ref[...].astype(F32).reshape(32, 2, 16, 128)
-    rows[...] = (got[:, 0] + got[:, 1]).reshape(512, 128)
+    rows[...] = got_ref[...].astype(F32)
     for a in range(4):
         mixed = rows[pl.ds(a, 128, stride=4), :]
         mean = jnp.mean(mixed, axis=0, keepdims=True)
@@ -140,16 +150,23 @@
         space=pltpu.HBM,
         limit=64 * 1024 * 1024 - 512 * 1024,
     )
-    got = lax.all_to_all(send.reshape(128, 8, 128), ("y", "z_lo", "x"), 0, 0, tiled=True).reshape(1024, 128)
+    got = lax.all_to_all(send.reshape(128, 8, 128), ("y", "x", "z_lo"), 0, 0, tiled=True).reshape(1024, 128)
     both = lax.all_gather(got, "core", axis=0, tiled=True)
     send = call(
         contract,
         jax.ShapeDtypeStruct((1024, 128), BF16),
-        [pltpu.VMEM((2, 256, 128), F32), pltpu.VMEM((16, 2, 32, 128), F32)],
+        [pltpu.VMEM((2, 256, 128), F32), pltpu.VMEM((4, 2, 2, 4, 16, 128), F32)],
         got,
         both,
     )
-    got = lax.all_to_all(send.reshape(256, 4, 128), ("y", "z_lo", "z_hi", "x"), 0, 0, tiled=True).reshape(1024, 128)
+    got = lax.all_to_all(send.reshape(16, 64, 128), ("z_lo", "z_hi"), 0, 0, tiled=True).reshape(1024, 128)
+    send = call(
+        add_halves,
+        jax.ShapeDtypeStruct((512, 128), BF16),
+        [pltpu.VMEM((8, 2, 32, 128), F32)],
+        got,
+    )
+    got = lax.all_to_all(send.reshape(16, 32, 128), ("y", "x"), 0, 0, tiled=True).reshape(512, 128)
     out = call(
         finish,
         jax.ShapeDtypeStruct((512, 128), BF16),

time: 83.9 us -> 87 us (1.037)
  the two profiles are of different devices: /device:TPU:1 before, /device:TPU:32 now
where the time goes in v3:
time: 87 us; the launch traced here: 86.7 us
  blocking collectives  82.3 us (95%)
  Pallas kernels  4.36 us (5%)
    all_to_all x1, blocking collectives, on_device(): lax.all_to_all(send.reshape(128, 8, 128), ('y', 'x', 'z_lo'), 0, 0, tiled...  39.4 us
    all_to_all x1, blocking collectives, on_device(): lax.all_to_all(send.reshape(16, 64, 128), ('z_lo', 'z_hi'), 0, 0, tiled=T...  29.9 us
    all_to_all x1, blocking collectives, on_device(): lax.all_to_all(send.reshape(16, 32, 128), ('y', 'x'), 0, 0, tiled=True)  10.9 us
    pallas_call x4, Pallas kernels, call(): pl.pallas_call(kernel, out_shape=outs, in_specs=[pl.BlockSpec(memory_spac...  4.36 us
    all_gather x1, blocking collectives, on_device(): both = lax.all_gather(got, 'core', axis=0, tiled=True)  2.17 us

profile of v3, /device:TPU:32, one launch (start us, length us, event | category | flops | bytes accessed | tf_op | source)
XLA Modules:
  0.0 86.7 jit_solution(10474615728822834353)
XLA Ops:
  0.0 2.8 %shard_map.118 = (bf16[1024,128]{1,0:T(8,128)(2,1)}, f32[512,128]{1,0:T(8,128)}, f32[2,128,128]{2,1,0:T(8,128)}, bf16[128,128]{1,0:T(8,128)(2,1)}) custom-call(bf16[512,128]{1,0:T(8,128)(2,1)} %bitcast.19, s32[8,64]{1,0:T(8,128)} %refs_1_.1, f32[1,128]{1,0:T(1,128)} %bitcast.20, f32[1,128]{1,0:T(1,128)} %bitcast.21, bf16[128,128]{1,0:T(8,128)(2,1)} %refs_4_.1, ...), custom_call_target="tpu_custom_call" | custom-call | tf_op jit(solution)/shard_map/pallas_call | solution.py:19
  2.8 39.4 %all_to_all.15 = bf16[128,8,128]{2,1,0:T(8,128)(2,1)S(1)} all-to-all(bf16[128,8,128]{2,1,0:T(8,128)(2,1)} %bitcast.18), channel_id=1, replica_groups=mesh['y'=4,'z_lo'=8,'core'=2,'z_hi'=2,'x'=4] {'y','x','z_lo'}, dimensions={0} | all-to-all | bytes 524288 | tf_op jit(solution)/shard_map/all_to_all | solution.py:153
  42.2 2.2 %all_gather.3.both_ref = bf16[2048,128]{1,0:T(8,128)(2,1)S(1)} all-gather(bf16[1024,128]{1,0:T(8,128)(2,1)S(1)} %bitcast.12), channel_id=1, replica_groups=mesh['y'=4,'z_lo'=8,'core'=2,'z_hi'=2,'x'=4] {'core'}, dimensions={0}, use_global_device_ids=true | all-gather | bytes 786432 | tf_op jit(solution)/shard_map/all_gather | solution.py:154
  44.3 0.6 shard_map.119
  44.9 29.9 %all_to_all.16 = bf16[16,64,128]{2,1,0:T(8,128)(2,1)S(1)} all-to-all(bf16[16,64,128]{2,1,0:T(8,128)(2,1)S(1)} %bitcast.15), channel_id=1, replica_groups=mesh['y'=4,'z_lo'=8,'core'=2,'z_hi'=2,'x'=4] {'z_lo','z_hi'}, dimensions={0} | all-to-all | bytes 524288 | tf_op jit(solution)/shard_map/all_to_all | solution.py:162
  74.8 0.0 copy-start
  74.8 0.1 shard_map.120
  74.8 0.0 copy-start.1
  74.9 0.0 copy-start.2
  74.9 10.9 %all_to_all.17 = bf16[16,32,128]{2,1,0:T(8,128)(2,1)S(1)} all-to-all(bf16[16,32,128]{2,1,0:T(8,128)(2,1)S(1)} %bitcast.16), channel_id=1, replica_groups=mesh['y'=4,'z_lo'=8,'core'=2,'z_hi'=2,'x'=4] {'y','x'}, dimensions={0} | all-to-all | bytes 262144 | tf_op jit(solution)/shard_map/all_to_all | solution.py:169
  85.7 0.0 copy-done
  85.7 0.0 copy-done.1
  85.7 0.0 copy-done.2
  85.8 1.0 %shard_map.121 = bf16[512,128]{1,0:T(8,128)(2,1)} custom-call(bf16[512,128]{1,0:T(8,128)(2,1)S(1)} %bitcast.17, f32[512,128]{1,0:T(8,128)S(1)} %copy-done, f32[2,128,128]{2,1,0:T(8,128)S(1)} %copy-done.1, bf16[128,128]{1,0:T(8,128)(2,1)S(1)} %copy-done.2), custom_call_target="tpu_custom_call" | custom-call | tf_op jit(solution)/shard_map/pallas_call | solution.py:19
Async XLA Ops:
  74.8 11.0 %copy-start = (f32[512,128]{1,0:T(8,128)S(1)}, f32[512,128]{1,0:T(8,128)}, u32[]{:S(2)}) copy-start(f32[512,128]{1,0:T(8,128)} %get-tuple-element.10.gating_ref) | copy-start | bytes 786436
  74.8 10.9 %copy-start.1 = (f32[2,128,128]{2,1,0:T(8,128)S(1)}, f32[2,128,128]{2,1,0:T(8,128)}, u32[]{:S(2)}) copy-start(f32[2,128,128]{2,1,0:T(8,128)} %get-tuple-element.11.affine_ref) | copy-start | bytes 393220
  74.9 10.9 %copy-start.2 = (bf16[128,128]{1,0:T(8,128)(2,1)S(1)}, bf16[128,128]{1,0:T(8,128)(2,1)}, u32[]{:S(2)}) copy-start(bf16[128,128]{1,0:T(8,128)(2,1)} %get-tuple-element.12.proj_ref) | copy-start | bytes 98308

commit v4 on v2

--- a/solution.py
+++ b/solution.py
@@ -9,6 +9,30 @@
 EPS = 1e-05
 F32, BF16 = jnp.float32, jnp.bfloat16
 VMEM_LIMIT = 32 * 1024 * 1024
+
+AXES = ("y", "z_lo", "core", "z_hi", "x")
+Z_IN = (3, 4, 2, 5, 1, 6, 0, 7)
+Z_OUT = (8, 7, 9, 6, 10, 5, 11, 4, 12, 3, 13, 2, 14, 1, 15, 0)
+AT_IN = tuple(Z_IN.index(z) for z in range(8))
+AT_OUT = tuple(Z_OUT.index(z) for z in range(16))
+
+
+def device(y, z, core, x):
+    return (((y * 8 + z % 8) * 2 + core) * 2 + z // 8) * 4 + x
+
+
+def peers(zs, core):
+    return [device(y, z, core, x) for z in zs for y in range(4) for x in range(4)]
+
+
+IN_GROUPS = [peers([z + 8 * half for z in Z_IN], core) for core in range(2) for half in range(2)]
+OUT_GROUPS = [peers(Z_OUT, core) for core in range(2)]
+
+
+def exchange(rows, groups):
+    count = len(groups[0])
+    chunks = rows.reshape(count, rows.shape[0] // count, 128)
+    return lax.all_to_all(chunks, AXES, 0, 0, axis_index_groups=groups, tiled=True).reshape(rows.shape)
 
 
 def dot_last(a, b):
@@ -63,13 +87,13 @@
 
 def contract(own_ref, both_ref, send_ref, lhs, out):
     own = own_ref[...].astype(F32).reshape(32, 4, 8, 128)
-    both = both_ref[...].astype(F32).reshape(2, 32, 4, 8, 128)
+    both = both_ref[...].astype(F32).reshape(2, 8, 4, 4, 8, 128)
     for x in range(2):
         lhs[x] = jnp.concatenate([own[:, 2 * x, :, :64], own[:, 2 * x + 1, :, :64]], axis=-1).reshape(256, 128)
     parts = []
     for x in range(4):
-        part = jnp.stack([both[0, :, x], both[1, :, x]], axis=1).reshape(512, 128)
-        parts.append(part[:, 64:])
+        part = [both[core, AT_IN[z], y, x] for y in range(4) for z in range(8) for core in range(2)]
+        parts.append(jnp.concatenate(part, axis=0)[:, 64:])
     rhs = jnp.concatenate(parts, axis=1).astype(BF16)
     mixed = []
     for e in range(2):
@@ -77,15 +101,18 @@
         mixed.append(dot_last(jnp.concatenate(halves, axis=1).astype(BF16), rhs))
     for h in range(8):
         at = slice(h * 64, (h + 1) * 64)
-        tile = jnp.concatenate([mixed[0][:, at], mixed[1][:, at]], axis=1).reshape(16, 8, 128)
-        out[:, 0, h * 4 : (h + 1) * 4, :] = tile[:, 0:4, :]
-        out[:, 1, h * 4 : (h + 1) * 4, :] = tile[:, 4:8, :]
+        tile = jnp.concatenate([mixed[0][:, at], mixed[1][:, at]], axis=1).reshape(8, 2, 8, 128)
+        to = slice(h % 4 * 4, h % 4 * 4 + 4)
+        for place, z in enumerate(Z_IN):
+            for s in range(2):
+                out[AT_OUT[h // 4 * 8 + z], :, s, to, :] = tile[place, :, 4 * s : 4 * s + 4, :]
     send_ref[...] = out[...].reshape(1024, 128).astype(BF16)
 
 
 def finish(got_ref, gating_ref, affine_ref, proj_ref, out_ref, rows):
-    got = got_ref[...].astype(F32).reshape(32, 2, 16, 128)
-    rows[...] = (got[:, 0] + got[:, 1]).reshape(512, 128)
+    got = got_ref[...].astype(F32).reshape(16, 64, 128)
+    for place, z in enumerate(Z_IN):
+        rows[place * 64 : (place + 1) * 64, :] = got[AT_OUT[z]] + got[AT_OUT[z + 8]]
     for a in range(4):
         mixed = rows[pl.ds(a, 128, stride=4), :]
         mean = jnp.mean(mixed, axis=0, keepdims=True)
@@ -140,16 +167,16 @@
         space=pltpu.HBM,
         limit=64 * 1024 * 1024 - 512 * 1024,
     )
-    got = lax.all_to_all(send.reshape(128, 8, 128), ("y", "z_lo", "x"), 0, 0, tiled=True).reshape(1024, 128)
+    got = exchange(send, IN_GROUPS)
     both = lax.all_gather(got, "core", axis=0, tiled=True)
     send = call(
         contract,
         jax.ShapeDtypeStruct((1024, 128), BF16),
-        [pltpu.VMEM((2, 256, 128), F32), pltpu.VMEM((16, 2, 32, 128), F32)],
+        [pltpu.VMEM((2, 256, 128), F32), pltpu.VMEM((16, 2, 2, 16, 128), F32)],
         got,
         both,
     )
-    got = lax.all_to_all(send.reshape(256, 4, 128), ("y", "z_lo", "z_hi", "x"), 0, 0, tiled=True).reshape(1024, 128)
+    got = exchange(send, OUT_GROUPS)
     out = call(
         finish,
         jax.ShapeDtypeStruct((512, 128), BF16),
@@ -163,7 +190,7 @@
 
 
 def solution(mesh):
-    fine = Mesh(mesh.devices.reshape(4, 8, 2, 2, 4), ("y", "z_lo", "core", "z_hi", "x"))
+    fine = Mesh(mesh.devices.reshape(4, 8, 2, 2, 4), AXES)
     res, ch = ("y", "z_lo", "core"), ("z_hi", "x")
     placed = (P(res, ch, None), P(res, ch)) + (P(),) * 10
     return jax.shard_map(on_device, mesh=fine, in_specs=placed, out_specs=P(res, ch, None), check_vma=False)

time: 83.9 us -> 76.4 us (0.911); the launches traced: 82.3 us -> 75.9 us
  blocking collectives: 77.9 us -> 71.6 us
    all_to_all x2, blocking collectives: 74.3 us -> 66.7 us  [exchange(): lax.all_to_all(chunks, AXES, 0, 0, axis_index_groups=groups, tiled=True)]
    all_gather x1, blocking collectives: 3.59 us -> 4.87 us  [on_device(): both = lax.all_gather(got, 'core', axis=0, tiled=True)]
where the time goes in v4:
time: 76.4 us; the launch traced here: 75.9 us
  blocking collectives  71.6 us (94%)
  Pallas kernels  4.29 us (6%)
    all_to_all x2, blocking collectives, exchange(): lax.all_to_all(chunks, AXES, 0, 0, axis_index_groups=groups, tiled=True)  66.7 us
    all_gather x1, blocking collectives, on_device(): both = lax.all_gather(got, 'core', axis=0, tiled=True)  4.87 us
    pallas_call x3, Pallas kernels, call(): pl.pallas_call(kernel, out_shape=outs, in_specs=[pl.BlockSpec(memory_spac...  4.29 us

profile of v4, /device:TPU:1, one launch (start us, length us, event | category | flops | bytes accessed | tf_op | source)
XLA Modules:
  0.0 75.9 jit_solution(17975169981162441824)
XLA Ops:
  0.0 2.8 %shard_map.118 = (bf16[1024,128]{1,0:T(8,128)(2,1)}, f32[512,128]{1,0:T(8,128)}, f32[2,128,128]{2,1,0:T(8,128)}, bf16[128,128]{1,0:T(8,128)(2,1)}) custom-call(bf16[512,128]{1,0:T(8,128)(2,1)} %bitcast.15, s32[8,64]{1,0:T(8,128)} %refs_1_.1, f32[1,128]{1,0:T(1,128)} %bitcast.16, f32[1,128]{1,0:T(1,128)} %bitcast.17, bf16[128,128]{1,0:T(8,128)(2,1)} %refs_4_.1, ...), custom_call_target="tpu_custom_call" | custom-call | tf_op jit(solution)/shard_map/pallas_call | solution.py:43
  2.8 36.0 %all_to_all.10 = bf16[128,8,128]{2,1,0:T(8,128)(2,1)S(1)} all-to-all(bf16[128,8,128]{2,1,0:T(8,128)(2,1)} %bitcast.14), channel_id=1, replica_groups={{48,49,50,51,176,177,178,179,304,305,306,307,432,433,434,435,64,65,66,6..., dimensions={0} | all-to-all | bytes 524288 | tf_op jit(solution)/shard_map/all_to_all | solution.py:35
  38.8 4.9 %all_gather.3.both_ref = bf16[2048,128]{1,0:T(8,128)(2,1)S(1)} all-gather(bf16[1024,128]{1,0:T(8,128)(2,1)S(1)} %bitcast.10), channel_id=1, replica_groups=mesh['y'=4,'z_lo'=8,'core'=2,'z_hi'=2,'x'=4] {'core'}, dimensions={0}, use_global_device_ids=true | all-gather | bytes 786432 | tf_op jit(solution)/shard_map/all_gather | solution.py:171
  43.7 0.5 shard_map.119
  44.2 0.0 copy-start
  44.2 0.0 copy-start.1
  44.2 0.0 copy-start.2
  44.3 30.6 %all_to_all.11 = bf16[256,4,128]{2,1,0:T(4,128)(2,1)S(1)} all-to-all(bf16[256,4,128]{2,1,0:T(4,128)(2,1)S(1)} %bitcast.13), channel_id=1, replica_groups={{4,5,6,7,132,133,134,135,260,261,262,263,388,389,390,391,112,113,114,11..., dimensions={0} | all-to-all | bytes 524288 | tf_op jit(solution)/shard_map/all_to_all | solution.py:35
  74.9 0.0 copy-done
  74.9 0.0 copy-done.1
  74.9 0.0 copy-done.2
  74.9 1.0 %shard_map.120 = bf16[512,128]{1,0:T(8,128)(2,1)} custom-call(bf16[1024,128]{1,0:T(8,128)(2,1)S(1)} %bitcast.12, f32[512,128]{1,0:T(8,128)S(1)} %copy-done, f32[2,128,128]{2,1,0:T(8,128)S(1)} %copy-done.1, bf16[128,128]{1,0:T(8,128)(2,1)S(1)} %copy-done.2), custom_call_target="tpu_custom_call" | custom-call | tf_op jit(solution)/shard_map/pallas_call | solution.py:43
Async XLA Ops:
  44.2 30.7 %copy-start = (f32[512,128]{1,0:T(8,128)S(1)}, f32[512,128]{1,0:T(8,128)}, u32[]{:S(2)}) copy-start(f32[512,128]{1,0:T(8,128)} %get-tuple-element.10.gating_ref) | copy-start | bytes 786436
  44.2 30.7 %copy-start.1 = (f32[2,128,128]{2,1,0:T(8,128)S(1)}, f32[2,128,128]{2,1,0:T(8,128)}, u32[]{:S(2)}) copy-start(f32[2,128,128]{2,1,0:T(8,128)} %get-tuple-element.11.affine_ref) | copy-start | bytes 393220
  44.2 30.7 %copy-start.2 = (bf16[128,128]{1,0:T(8,128)(2,1)S(1)}, bf16[128,128]{1,0:T(8,128)(2,1)}, u32[]{:S(2)}) copy-start(bf16[128,128]{1,0:T(8,128)(2,1)} %get-tuple-element.12.proj_ref) | copy-start | bytes 98308

commit v5 on v4

--- a/solution.py
+++ b/solution.py
@@ -12,7 +12,7 @@
 
 AXES = ("y", "z_lo", "core", "z_hi", "x")
 Z_IN = (3, 4, 2, 5, 1, 6, 0, 7)
-Z_OUT = (8, 7, 9, 6, 10, 5, 11, 4, 12, 3, 13, 2, 14, 1, 15, 0)
+Z_OUT = (8, 9, 7, 10, 6, 11, 5, 12, 13, 4, 14, 15, 3, 2, 1, 0)
 AT_IN = tuple(Z_IN.index(z) for z in range(8))
 AT_OUT = tuple(Z_OUT.index(z) for z in range(16))
 
@@ -22,7 +22,7 @@
 
 
 def peers(zs, core):
-    return [device(y, z, core, x) for z in zs for y in range(4) for x in range(4)]
+    return [device(y, z, core, x) for z in zs for y in (3, 2, 1, 0) for x in (3, 2, 1, 0)]
 
 
 IN_GROUPS = [peers([z + 8 * half for z in Z_IN], core) for core in range(2) for half in range(2)]
@@ -92,7 +92,7 @@
         lhs[x] = jnp.concatenate([own[:, 2 * x, :, :64], own[:, 2 * x + 1, :, :64]], axis=-1).reshape(256, 128)
     parts = []
     for x in range(4):
-        part = [both[core, AT_IN[z], y, x] for y in range(4) for z in range(8) for core in range(2)]
+        part = [both[core, AT_IN[z], 3 - y, x] for y in range(4) for z in range(8) for core in range(2)]
         parts.append(jnp.concatenate(part, axis=0)[:, 64:])
     rhs = jnp.concatenate(parts, axis=1).astype(BF16)
     mixed = []
@@ -102,7 +102,7 @@
     for h in range(8):
         at = slice(h * 64, (h + 1) * 64)
         tile = jnp.concatenate([mixed[0][:, at], mixed[1][:, at]], axis=1).reshape(8, 2, 8, 128)
-        to = slice(h % 4 * 4, h % 4 * 4 + 4)
+        to = slice(12 - h % 4 * 4, 16 - h % 4 * 4)
         for place, z in enumerate(Z_IN):
             for s in range(2):
                 out[AT_OUT[h // 4 * 8 + z], :, s, to, :] = tile[place, :, 4 * s : 4 * s + 4, :]
@@ -155,17 +155,16 @@
     send, gating, affine, last = call(
         prepare,
         (
-            jax.ShapeDtypeStruct((1024, 128), BF16),
-            jax.ShapeDtypeStruct((512, 128), F32),
-            jax.ShapeDtypeStruct((2, 128, 128), F32),
-            jax.ShapeDtypeStruct((128, 128), BF16),
+            pltpu.VMEM((1024, 128), BF16),
+            pltpu.VMEM((512, 128), F32),
+            pltpu.VMEM((2, 128, 128), F32),
+            pltpu.VMEM((128, 128), BF16),
         ),
         [pltpu.VMEM((128, 8, 128), F32)]
         + [pltpu.VMEM(o.shape, o.dtype) for o in operands]
         + [pltpu.SemaphoreType.DMA((len(operands),))],
-        *operands,
+        *[pltpu.with_memory_space_constraint(operand, pltpu.HBM) for operand in operands],
         space=pltpu.HBM,
-        limit=64 * 1024 * 1024 - 512 * 1024,
     )
     got = exchange(send, IN_GROUPS)
     both = lax.all_gather(got, "core", axis=0, tiled=True)

time: 76.4 us -> 72.6 us (0.950)
  blocking collectives: 71.6 us -> 68.9 us
  Pallas kernels: 4.29 us -> 3.48 us
    all_to_all x2, blocking collectives: 66.7 us -> 63.8 us  [exchange(): lax.all_to_all(chunks, AXES, 0, 0, axis_index_groups=groups, tiled=True)]
    pallas_call x3, Pallas kernels: 4.29 us -> 3.48 us  [call(): pl.pallas_call(kernel, out_shape=outs, in_specs=[pl.BlockSpec(memory_spac...]
where the time goes in v5:
time: 72.6 us; the launch traced here: 72.4 us
  blocking collectives  68.9 us (95%)
  Pallas kernels  3.48 us (5%)
    all_to_all x2, blocking collectives, exchange(): lax.all_to_all(chunks, AXES, 0, 0, axis_index_groups=groups, tiled=True)  63.8 us
    all_gather x1, blocking collectives, on_device(): both = lax.all_gather(got, 'core', axis=0, tiled=True)  5.09 us
    pallas_call x3, Pallas kernels, call(): pl.pallas_call(kernel, out_shape=outs, in_specs=[pl.BlockSpec(memory_spac...  3.48 us

profile of v5, /device:TPU:1, one launch (start us, length us, event | category | flops | bytes accessed | tf_op | source)
XLA Modules:
  0.0 72.4 jit_solution(1665090014659007780)
XLA Ops:
  0.0 2.0 %shard_map.118 = (bf16[1024,128]{1,0:T(8,128)(2,1)S(1)}, f32[512,128]{1,0:T(8,128)S(1)}, f32[2,128,128]{2,1,0:T(8,128)S(1)}, bf16[128,128]{1,0:T(8,128)(2,1)S(1)}) custom-call(bf16[512,128]{1,0:T(8,128)(2,1)} %bitcast.15, s32[8,64]{1,0:T(8,128)} %refs_1_.1, f32[1,128]{1,0:T(1,128)} %bitcast.16, f32[1,128]{1,0:T(1,128)} %bitcast.17, ...), custom_call_target="tpu_custom_call" | custom-call | tf_op jit(solution)/shard_map/pallas_call | solution.py:43
  2.0 33.5 %all_to_all.10 = bf16[128,8,128]{2,1,0:T(8,128)(2,1)S(1)} all-to-all(bf16[128,8,128]{2,1,0:T(8,128)(2,1)S(1)} %bitcast.14), channel_id=1, replica_groups={{435,434,433,432,307,306,305,304,179,178,177,176,51,50,49,48,451,450,44..., dimensions={0} | all-to-all | bytes 524288 | tf_op jit(solution)/shard_map/all_to_all | solution.py:35
  35.5 5.1 %all_gather.3.both_ref = bf16[2048,128]{1,0:T(8,128)(2,1)S(1)} all-gather(bf16[1024,128]{1,0:T(8,128)(2,1)S(1)} %bitcast.10), channel_id=1, replica_groups=mesh['y'=4,'z_lo'=8,'core'=2,'z_hi'=2,'x'=4] {'core'}, dimensions={0}, use_global_device_ids=true | all-gather | bytes 786432 | tf_op jit(solution)/shard_map/all_gather | solution.py:170
  40.6 0.5 shard_map.119
  41.1 30.3 %all_to_all.11 = bf16[256,4,128]{2,1,0:T(4,128)(2,1)S(1)} all-to-all(bf16[256,4,128]{2,1,0:T(4,128)(2,1)S(1)} %bitcast.13), channel_id=1, replica_groups={{391,390,389,388,263,262,261,260,135,134,133,132,7,6,5,4,407,406,405,40..., dimensions={0} | all-to-all | bytes 524288 | tf_op jit(solution)/shard_map/all_to_all | solution.py:35
  71.4 1.0 %shard_map.120 = bf16[512,128]{1,0:T(8,128)(2,1)} custom-call(bf16[1024,128]{1,0:T(8,128)(2,1)S(1)} %bitcast.12, f32[512,128]{1,0:T(8,128)S(1)} %get-tuple-element.10.gating_ref, f32[2,128,128]{2,1,0:T(8,128)S(1)} %get-tuple-element.11.affine_ref, bf16[128,128]{1,0:T(8,128)(2,1)S(1)} %get-tuple-element.12.proj_ref), custom_call_target="tpu_custom_call" | custom-call | tf_op jit(solution)/shard_map/pallas_call | solution.py:43

commit v6 on v5

--- a/solution.py
+++ b/solution.py
@@ -11,9 +11,9 @@
 VMEM_LIMIT = 32 * 1024 * 1024
 
 AXES = ("y", "z_lo", "core", "z_hi", "x")
-Z_IN = (3, 4, 2, 5, 1, 6, 0, 7)
+Z_IN = ((4, 3, 5, 2, 6, 1, 7, 0), (3, 4, 2, 5, 1, 6, 7, 0))
 Z_OUT = (8, 9, 7, 10, 6, 11, 5, 12, 13, 4, 14, 15, 3, 2, 1, 0)
-AT_IN = tuple(Z_IN.index(z) for z in range(8))
+AT_IN = tuple(tuple(order.index(z) for z in range(8)) for order in Z_IN)
 AT_OUT = tuple(Z_OUT.index(z) for z in range(16))
 
 
@@ -25,7 +25,7 @@
     return [device(y, z, core, x) for z in zs for y in (3, 2, 1, 0) for x in (3, 2, 1, 0)]
 
 
-IN_GROUPS = [peers([z + 8 * half for z in Z_IN], core) for core in range(2) for half in range(2)]
+IN_GROUPS = [peers([z + 8 * half for z in Z_IN[half]], core) for core in range(2) for half in range(2)]
 OUT_GROUPS = [peers(Z_OUT, core) for core in range(2)]
 
 
@@ -86,13 +86,22 @@
 
 
 def contract(own_ref, both_ref, send_ref, lhs, out):
-    own = own_ref[...].astype(F32).reshape(32, 4, 8, 128)
-    both = both_ref[...].astype(F32).reshape(2, 8, 4, 4, 8, 128)
-    for x in range(2):
-        lhs[x] = jnp.concatenate([own[:, 2 * x, :, :64], own[:, 2 * x + 1, :, :64]], axis=-1).reshape(256, 128)
+    half = lax.axis_index("z_hi")
+
+    def block(ref, core, z):
+        place = jnp.where(half == 0, AT_IN[0][z], AT_IN[1][z])
+        at = pl.multiple_of(core * 1024 + place * 128, 128)
+        return ref[pl.ds(at, 128), :].astype(F32).reshape(4, 4, 8, 128)
+
+    for z in range(8):
+        own = block(own_ref, 0, z)
+        for x in range(2):
+            pair = jnp.concatenate([own[:, 2 * x, :, :64], own[:, 2 * x + 1, :, :64]], axis=-1)
+            lhs[x, z * 32 : (z + 1) * 32, :] = pair.reshape(32, 128)
+    both = [[block(both_ref, core, z) for z in range(8)] for core in range(2)]
     parts = []
     for x in range(4):
-        part = [both[core, AT_IN[z], 3 - y, x] for y in range(4) for z in range(8) for core in range(2)]
+        part = [both[core][z][3 - y, x] for y in range(4) for z in range(8) for core in range(2)]
         parts.append(jnp.concatenate(part, axis=0)[:, 64:])
     rhs = jnp.concatenate(parts, axis=1).astype(BF16)
     mixed = []
@@ -103,16 +112,17 @@
         at = slice(h * 64, (h + 1) * 64)
         tile = jnp.concatenate([mixed[0][:, at], mixed[1][:, at]], axis=1).reshape(8, 2, 8, 128)
         to = slice(12 - h % 4 * 4, 16 - h % 4 * 4)
-        for place, z in enumerate(Z_IN):
+        for z in range(8):
             for s in range(2):
-                out[AT_OUT[h // 4 * 8 + z], :, s, to, :] = tile[place, :, 4 * s : 4 * s + 4, :]
+                out[AT_OUT[h // 4 * 8 + z], :, s, to, :] = tile[z, :, 4 * s : 4 * s + 4, :]
     send_ref[...] = out[...].reshape(1024, 128).astype(BF16)
 
 
 def finish(got_ref, gating_ref, affine_ref, proj_ref, out_ref, rows):
     got = got_ref[...].astype(F32).reshape(16, 64, 128)
-    for place, z in enumerate(Z_IN):
-        rows[place * 64 : (place + 1) * 64, :] = got[AT_OUT[z]] + got[AT_OUT[z + 8]]
+    for place in range(8):
+        low, high = Z_IN[0][place], Z_IN[1][place] + 8
+        rows[place * 64 : (place + 1) * 64, :] = got[AT_OUT[low]] + got[AT_OUT[high]]
     for a in range(4):
         mixed = rows[pl.ds(a, 128, stride=4), :]
         mean = jnp.mean(mixed, axis=0, keepdims=True)

time: 72.6 us -> 71.3 us (0.982)
  blocking collectives: 68.9 us -> 67.6 us
    all_to_all x2, blocking collectives: 63.8 us -> 62.7 us  [exchange(): lax.all_to_all(chunks, AXES, 0, 0, axis_index_groups=groups, tiled=True)]
where the time goes in v6:
time: 71.3 us; the launch traced here: 71.1 us
  blocking collectives  67.6 us (95%)
  Pallas kernels  3.48 us (5%)
    all_to_all x2, blocking collectives, exchange(): lax.all_to_all(chunks, AXES, 0, 0, axis_index_groups=groups, tiled=True)  62.7 us
    all_gather x1, blocking collectives, on_device(): both = lax.all_gather(got, 'core', axis=0, tiled=True)  4.94 us
    pallas_call x3, Pallas kernels, call(): pl.pallas_call(kernel, out_shape=outs, in_specs=[pl.BlockSpec(memory_spac...  3.48 us

profile of v6, /device:TPU:1, one launch (start us, length us, event | category | flops | bytes accessed | tf_op | source)
XLA Modules:
  0.0 71.1 jit_solution(2337316114760633479)
XLA Ops:
  0.0 2.0 %shard_map.118 = (bf16[1024,128]{1,0:T(8,128)(2,1)S(1)}, f32[512,128]{1,0:T(8,128)S(1)}, f32[2,128,128]{2,1,0:T(8,128)S(1)}, bf16[128,128]{1,0:T(8,128)(2,1)S(1)}) custom-call(bf16[512,128]{1,0:T(8,128)(2,1)} %bitcast.15, s32[8,64]{1,0:T(8,128)} %refs_1_.1, f32[1,128]{1,0:T(1,128)} %bitcast.16, f32[1,128]{1,0:T(1,128)} %bitcast.17, ...), custom_call_target="tpu_custom_call" | custom-call | tf_op jit(solution)/shard_map/pallas_call | solution.py:43
  2.0 31.8 %all_to_all.10 = bf16[128,8,128]{2,1,0:T(8,128)(2,1)S(1)} all-to-all(bf16[128,8,128]{2,1,0:T(8,128)(2,1)S(1)} %bitcast.14), channel_id=1, replica_groups={{451,450,449,448,323,322,321,320,195,194,193,192,67,66,65,64,435,434,43..., dimensions={0} | all-to-all | bytes 524288 | tf_op jit(solution)/shard_map/all_to_all | solution.py:35
  33.7 4.9 %all_gather.3.both_ref = bf16[2048,128]{1,0:T(8,128)(2,1)S(1)} all-gather(bf16[1024,128]{1,0:T(8,128)(2,1)S(1)} %bitcast.10), channel_id=1, replica_groups=mesh['y'=4,'z_lo'=8,'core'=2,'z_hi'=2,'x'=4] {'core'}, dimensions={0}, use_global_device_ids=true | all-gather | bytes 786432 | tf_op jit(solution)/shard_map/all_gather | solution.py:180
  38.7 0.5 shard_map.119
  39.2 30.9 %all_to_all.11 = bf16[256,4,128]{2,1,0:T(4,128)(2,1)S(1)} all-to-all(bf16[256,4,128]{2,1,0:T(4,128)(2,1)S(1)} %bitcast.13), channel_id=1, replica_groups={{391,390,389,388,263,262,261,260,135,134,133,132,7,6,5,4,407,406,405,40..., dimensions={0} | all-to-all | bytes 524288 | tf_op jit(solution)/shard_map/all_to_all | solution.py:35
  70.1 1.0 %shard_map.120 = bf16[512,128]{1,0:T(8,128)(2,1)} custom-call(bf16[1024,128]{1,0:T(8,128)(2,1)S(1)} %bitcast.12, f32[512,128]{1,0:T(8,128)S(1)} %get-tuple-element.10.gating_ref, f32[2,128,128]{2,1,0:T(8,128)S(1)} %get-tuple-element.11.affine_ref, bf16[128,128]{1,0:T(8,128)(2,1)S(1)} %get-tuple-element.12.proj_ref), custom_call_target="tpu_custom_call" | custom-call | tf_op jit(solution)/shard_map/pallas_call | solution.py:43

commit v7 on v6

--- a/solution.py
+++ b/solution.py
@@ -11,7 +11,7 @@
 VMEM_LIMIT = 32 * 1024 * 1024
 
 AXES = ("y", "z_lo", "core", "z_hi", "x")
-Z_IN = ((4, 3, 5, 2, 6, 1, 7, 0), (3, 4, 2, 5, 1, 6, 7, 0))
+Z_IN = ((5, 4, 3, 6, 2, 1, 7, 0), (3, 4, 2, 5, 6, 1, 7, 0))
 Z_OUT = (8, 9, 7, 10, 6, 11, 5, 12, 13, 4, 14, 15, 3, 2, 1, 0)
 AT_IN = tuple(tuple(order.index(z) for z in range(8)) for order in Z_IN)
 AT_OUT = tuple(Z_OUT.index(z) for z in range(16))

time: 71.3 us -> 71.3 us (level)
    all_gather x1, blocking collectives: 4.94 us -> 2.6 us  [on_device(): both = lax.all_gather(got, 'core', axis=0, tiled=True)]
    all_to_all x2, blocking collectives: 62.7 us -> 65 us  [exchange(): lax.all_to_all(chunks, AXES, 0, 0, axis_index_groups=groups, tiled=True)]
where the time goes in v7:
time: 71.3 us; the launch traced here: 71.1 us
  blocking collectives  67.6 us (95%)
  Pallas kernels  3.48 us (5%)
    all_to_all x2, blocking collectives, exchange(): lax.all_to_all(chunks, AXES, 0, 0, axis_index_groups=groups, tiled=True)  65 us
    pallas_call x3, Pallas kernels, call(): pl.pallas_call(kernel, out_shape=outs, in_specs=[pl.BlockSpec(memory_spac...  3.48 us
    all_gather x1, blocking collectives, on_device(): both = lax.all_gather(got, 'core', axis=0, tiled=True)  2.6 us

profile of v7, /device:TPU:1, one launch (start us, length us, event | category | flops | bytes accessed | tf_op | source)
XLA Modules:
  0.0 71.1 jit_solution(3458125440119814997)
XLA Ops:
  0.0 2.0 %shard_map.118 = (bf16[1024,128]{1,0:T(8,128)(2,1)S(1)}, f32[512,128]{1,0:T(8,128)S(1)}, f32[2,128,128]{2,1,0:T(8,128)S(1)}, bf16[128,128]{1,0:T(8,128)(2,1)S(1)}) custom-call(bf16[512,128]{1,0:T(8,128)(2,1)} %bitcast.15, s32[8,64]{1,0:T(8,128)} %refs_1_.1, f32[1,128]{1,0:T(1,128)} %bitcast.16, f32[1,128]{1,0:T(1,128)} %bitcast.17, ...), custom_call_target="tpu_custom_call" | custom-call | tf_op jit(solution)/shard_map/pallas_call | solution.py:43
  2.0 33.5 %all_to_all.10 = bf16[128,8,128]{2,1,0:T(8,128)(2,1)S(1)} all-to-all(bf16[128,8,128]{2,1,0:T(8,128)(2,1)S(1)} %bitcast.14), channel_id=1, replica_groups={{467,466,465,464,339,338,337,336,211,210,209,208,83,82,81,80,451,450,44..., dimensions={0} | all-to-all | bytes 524288 | tf_op jit(solution)/shard_map/all_to_all | solution.py:35
  35.5 2.6 %all_gather.3.both_ref = bf16[2048,128]{1,0:T(8,128)(2,1)S(1)} all-gather(bf16[1024,128]{1,0:T(8,128)(2,1)S(1)} %bitcast.10), channel_id=1, replica_groups=mesh['y'=4,'z_lo'=8,'core'=2,'z_hi'=2,'x'=4] {'core'}, dimensions={0}, use_global_device_ids=true | all-gather | bytes 786432 | tf_op jit(solution)/shard_map/all_gather | solution.py:180
  38.1 0.5 shard_map.119
  38.6 31.5 %all_to_all.11 = bf16[256,4,128]{2,1,0:T(4,128)(2,1)S(1)} all-to-all(bf16[256,4,128]{2,1,0:T(4,128)(2,1)S(1)} %bitcast.13), channel_id=1, replica_groups={{391,390,389,388,263,262,261,260,135,134,133,132,7,6,5,4,407,406,405,40..., dimensions={0} | all-to-all | bytes 524288 | tf_op jit(solution)/shard_map/all_to_all | solution.py:35
  70.1 1.0 %shard_map.120 = bf16[512,128]{1,0:T(8,128)(2,1)} custom-call(bf16[1024,128]{1,0:T(8,128)(2,1)S(1)} %bitcast.12, f32[512,128]{1,0:T(8,128)S(1)} %get-tuple-element.10.gating_ref, f32[2,128,128]{2,1,0:T(8,128)S(1)} %get-tuple-element.11.affine_ref, bf16[128,128]{1,0:T(8,128)(2,1)S(1)} %get-tuple-element.12.proj_ref), custom_call_target="tpu_custom_call" | custom-call | tf_op jit(solution)/shard_map/pallas_call | solution.py:43

commit v8 on v6

--- a/solution.py
+++ b/solution.py
@@ -39,12 +39,13 @@
     return lax.dot_general(a, b, (((1,), (1,)), ((), ())), preferred_element_type=F32)
 
 
-def call(kernel, outs, scratch, *args, space=pltpu.VMEM, limit=VMEM_LIMIT):
+def call(kernel, outs, scratch, *args, space=pltpu.VMEM, limit=VMEM_LIMIT, out=None):
     return pl.pallas_call(
         kernel,
         out_shape=outs,
         in_specs=[pl.BlockSpec(memory_space=space)] * len(args),
         scratch_shapes=scratch,
+        **({} if out is None else dict(out_specs=pl.BlockSpec(memory_space=out))),
         compiler_params=pltpu.CompilerParams(vmem_limit_bytes=limit),
     )(*args)
 
@@ -118,11 +119,12 @@
     send_ref[...] = out[...].reshape(1024, 128).astype(BF16)
 
 
-def finish(got_ref, gating_ref, affine_ref, proj_ref, out_ref, rows):
+def finish(got_ref, gating_ref, affine_ref, proj_ref, out_ref, rows, done, sems):
     got = got_ref[...].astype(F32).reshape(16, 64, 128)
     for place in range(8):
         low, high = Z_IN[0][place], Z_IN[1][place] + 8
         rows[place * 64 : (place + 1) * 64, :] = got[AT_OUT[low]] + got[AT_OUT[high]]
+    copies = []
     for a in range(4):
         mixed = rows[pl.ds(a, 128, stride=4), :]
         mean = jnp.mean(mixed, axis=0, keepdims=True)
@@ -130,8 +132,12 @@
         spread = jnp.mean(centred * centred, axis=0, keepdims=True)
         normed = (centred * lax.rsqrt(spread + EPS) * affine_ref[0] + affine_ref[1]).astype(BF16)
         projected = lax.dot_general(normed, proj_ref[...], (((0,), (0,)), ((), ())), preferred_element_type=F32)
-        at = slice(a * 128, (a + 1) * 128)
-        out_ref[at, :] = (gating_ref[at, :] * projected).astype(BF16)
+        at = pl.ds(a * 128, 128)
+        done[at, :] = (gating_ref[at, :] * projected).astype(BF16)
+        copies.append(pltpu.make_async_copy(done.at[at, :], out_ref.at[at, :], sems.at[a]))
+        copies[-1].start()
+    for copy in copies:
+        copy.wait()
 
 
 def on_device(
@@ -189,11 +195,12 @@
     out = call(
         finish,
         jax.ShapeDtypeStruct((512, 128), BF16),
-        [pltpu.VMEM((512, 128), F32)],
+        [pltpu.VMEM((512, 128), F32), pltpu.VMEM((512, 128), BF16), pltpu.SemaphoreType.DMA((4,))],
         got,
         gating,
         affine,
         last,
+        out=pltpu.HBM,
     )
     return out.reshape(8, 64, 128)
 

time: 71.3 us -> 71.3 us (level)
  no operation moved by 1% of the time
where the time goes in v8:
time: 71.3 us; the launch traced here: 71.1 us
  blocking collectives  67.6 us (95%)
  Pallas kernels  3.49 us (5%)
    all_to_all x2, blocking collectives, exchange(): lax.all_to_all(chunks, AXES, 0, 0, axis_index_groups=groups, tiled=True)  62.7 us
    all_gather x1, blocking collectives, on_device(): both = lax.all_gather(got, 'core', axis=0, tiled=True)  4.94 us
    pallas_call x3, Pallas kernels, call(): pl.pallas_call(kernel, out_shape=outs, in_specs=[pl.BlockSpec(memory_spac...  3.49 us

profile of v8, /device:TPU:1, one launch (start us, length us, event | category | flops | bytes accessed | tf_op | source)
XLA Modules:
  0.0 71.1 jit_solution(10311163552725928843)
XLA Ops:
  0.0 2.0 %shard_map.118 = (bf16[1024,128]{1,0:T(8,128)(2,1)S(1)}, f32[512,128]{1,0:T(8,128)S(1)}, f32[2,128,128]{2,1,0:T(8,128)S(1)}, bf16[128,128]{1,0:T(8,128)(2,1)S(1)}) custom-call(bf16[512,128]{1,0:T(8,128)(2,1)} %bitcast.15, s32[8,64]{1,0:T(8,128)} %refs_1_.1, f32[1,128]{1,0:T(1,128)} %bitcast.16, f32[1,128]{1,0:T(1,128)} %bitcast.17, ...), custom_call_target="tpu_custom_call" | custom-call | tf_op jit(solution)/shard_map/pallas_call | solution.py:43
  2.0 31.8 %all_to_all.10 = bf16[128,8,128]{2,1,0:T(8,128)(2,1)S(1)} all-to-all(bf16[128,8,128]{2,1,0:T(8,128)(2,1)S(1)} %bitcast.14), channel_id=1, replica_groups={{451,450,449,448,323,322,321,320,195,194,193,192,67,66,65,64,435,434,43..., dimensions={0} | all-to-all | bytes 524288 | tf_op jit(solution)/shard_map/all_to_all | solution.py:35
  33.7 4.9 %all_gather.3.both_ref = bf16[2048,128]{1,0:T(8,128)(2,1)S(1)} all-gather(bf16[1024,128]{1,0:T(8,128)(2,1)S(1)} %bitcast.10), channel_id=1, replica_groups=mesh['y'=4,'z_lo'=8,'core'=2,'z_hi'=2,'x'=4] {'core'}, dimensions={0}, use_global_device_ids=true | all-gather | bytes 786432 | tf_op jit(solution)/shard_map/all_gather | solution.py:186
  38.7 0.5 shard_map.119
  39.2 30.9 %all_to_all.11 = bf16[256,4,128]{2,1,0:T(4,128)(2,1)S(1)} all-to-all(bf16[256,4,128]{2,1,0:T(4,128)(2,1)S(1)} %bitcast.13), channel_id=1, replica_groups={{391,390,389,388,263,262,261,260,135,134,133,132,7,6,5,4,407,406,405,40..., dimensions={0} | all-to-all | bytes 524288 | tf_op jit(solution)/shard_map/all_to_all | solution.py:35
  70.1 1.0 %shard_map.120 = bf16[512,128]{1,0:T(8,128)(2,1)} custom-call(bf16[1024,128]{1,0:T(8,128)(2,1)S(1)} %bitcast.12, f32[512,128]{1,0:T(8,128)S(1)} %get-tuple-element.10.gating_ref, f32[2,128,128]{2,1,0:T(8,128)S(1)} %get-tuple-element.11.affine_ref, bf16[128,128]{1,0:T(8,128)(2,1)S(1)} %get-tuple-element.12.proj_ref), custom_call_target="tpu_custom_call" | custom-call | tf_op jit(solution)/shard_map/pallas_call | solution.py:43

commit v9 on v7

--- a/solution.py
+++ b/solution.py
@@ -11,7 +11,7 @@
 VMEM_LIMIT = 32 * 1024 * 1024
 
 AXES = ("y", "z_lo", "core", "z_hi", "x")
-Z_IN = ((5, 4, 3, 6, 2, 1, 7, 0), (3, 4, 2, 5, 6, 1, 7, 0))
+Z_IN = ((4, 3, 5, 2, 6, 1, 7, 0), (3, 4, 2, 5, 6, 1, 7, 0))
 Z_OUT = (8, 9, 7, 10, 6, 11, 5, 12, 13, 4, 14, 15, 3, 2, 1, 0)
 AT_IN = tuple(tuple(order.index(z) for z in range(8)) for order in Z_IN)
 AT_OUT = tuple(Z_OUT.index(z) for z in range(16))

time: 71.3 us -> 71.3 us (level)
    all_gather x1, blocking collectives: 2.6 us -> 4.94 us  [on_device(): both = lax.all_gather(got, 'core', axis=0, tiled=True)]
    all_to_all x2, blocking collectives: 65 us -> 62.7 us  [exchange(): lax.all_to_all(chunks, AXES, 0, 0, axis_index_groups=groups, tiled=True)]
where the time goes in v9:
time: 71.3 us; the launch traced here: 71.1 us
  blocking collectives  67.6 us (95%)
  Pallas kernels  3.48 us (5%)
    all_to_all x2, blocking collectives, exchange(): lax.all_to_all(chunks, AXES, 0, 0, axis_index_groups=groups, tiled=True)  62.7 us
    all_gather x1, blocking collectives, on_device(): both = lax.all_gather(got, 'core', axis=0, tiled=True)  4.94 us
    pallas_call x3, Pallas kernels, call(): pl.pallas_call(kernel, out_shape=outs, in_specs=[pl.BlockSpec(memory_spac...  3.48 us

profile of v9, /device:TPU:1, one launch (start us, length us, event | category | flops | bytes accessed | tf_op | source)
XLA Modules:
  0.0 71.1 jit_solution(6319218404020189214)
XLA Ops:
  0.0 2.0 %shard_map.118 = (bf16[1024,128]{1,0:T(8,128)(2,1)S(1)}, f32[512,128]{1,0:T(8,128)S(1)}, f32[2,128,128]{2,1,0:T(8,128)S(1)}, bf16[128,128]{1,0:T(8,128)(2,1)S(1)}) custom-call(bf16[512,128]{1,0:T(8,128)(2,1)} %bitcast.15, s32[8,64]{1,0:T(8,128)} %refs_1_.1, f32[1,128]{1,0:T(1,128)} %bitcast.16, f32[1,128]{1,0:T(1,128)} %bitcast.17, ...), custom_call_target="tpu_custom_call" | custom-call | tf_op jit(solution)/shard_map/pallas_call | solution.py:43
  2.0 31.8 %all_to_all.10 = bf16[128,8,128]{2,1,0:T(8,128)(2,1)S(1)} all-to-all(bf16[128,8,128]{2,1,0:T(8,128)(2,1)S(1)} %bitcast.14), channel_id=1, replica_groups={{451,450,449,448,323,322,321,320,195,194,193,192,67,66,65,64,435,434,43..., dimensions={0} | all-to-all | bytes 524288 | tf_op jit(solution)/shard_map/all_to_all | solution.py:35
  33.7 4.9 %all_gather.3.both_ref = bf16[2048,128]{1,0:T(8,128)(2,1)S(1)} all-gather(bf16[1024,128]{1,0:T(8,128)(2,1)S(1)} %bitcast.10), channel_id=1, replica_groups=mesh['y'=4,'z_lo'=8,'core'=2,'z_hi'=2,'x'=4] {'core'}, dimensions={0}, use_global_device_ids=true | all-gather | bytes 786432 | tf_op jit(solution)/shard_map/all_gather | solution.py:180
  38.7 0.5 shard_map.119
  39.2 30.9 %all_to_all.11 = bf16[256,4,128]{2,1,0:T(4,128)(2,1)S(1)} all-to-all(bf16[256,4,128]{2,1,0:T(4,128)(2,1)S(1)} %bitcast.13), channel_id=1, replica_groups={{391,390,389,388,263,262,261,260,135,134,133,132,7,6,5,4,407,406,405,40..., dimensions={0} | all-to-all | bytes 524288 | tf_op jit(solution)/shard_map/all_to_all | solution.py:35
  70.1 1.0 %shard_map.120 = bf16[512,128]{1,0:T(8,128)(2,1)} custom-call(bf16[1024,128]{1,0:T(8,128)(2,1)S(1)} %bitcast.12, f32[512,128]{1,0:T(8,128)S(1)} %get-tuple-element.10.gating_ref, f32[2,128,128]{2,1,0:T(8,128)S(1)} %get-tuple-element.11.affine_ref, bf16[128,128]{1,0:T(8,128)(2,1)S(1)} %get-tuple-element.12.proj_ref), custom_call_target="tpu_custom_call" | custom-call | tf_op jit(solution)/shard_map/pallas_call | solution.py:43
